TPU v7x, 32 devices: a whole 2x2x4 slice. The times are simulated.
32 devices in a mesh: dp: 4 (over y, x), tensor: 2 (over core), seq: 4 (over z).
Axes of the slice: x: 2, y: 2, z: 4, core: 2. Of those that a mesh axis runs over, the one named last changes fastest.
Arguments:
- tokens: bfloat16 [8, 1024, 1472], P(('dp', 'tensor'), 'seq'), may hold values from -6 to 6
- segment_ids: int32 [8, 1024], P('dp'), may hold values from 0 to 7, never falling along the last dimension, each value on 1 to 896 neighbouring positions
- buckets: int32 [2047], replicated, may hold values from 0 to 31, as said below
- gain_attn: bfloat16 [1472], replicated, may hold values from 0.5 to 1.5
- w_query: bfloat16 [1472, 384], P(None, 'tensor'), may hold values from -0.078125 to 0.078125
- w_key: bfloat16 [1472, 384], P(None, 'tensor'), may hold values from -0.078125 to 0.078125
- w_value: bfloat16 [1472, 384], P(None, 'tensor'), may hold values from -0.15625 to 0.15625
- w_out: bfloat16 [1472, 384], P(None, 'tensor'), may hold values from -1.25 to 1.25
- rel_table: bfloat16 [32, 6], P(None, 'tensor'), may hold values from -4 to 4
- gain_ff: bfloat16 [1472], replicated, may hold values from 0.5 to 1.5
- w_gate: bfloat16 [1472, 3584], P(None, 'tensor'), may hold values from -0.15625 to 0.15625
- w_up: bfloat16 [1472, 3584], P(None, 'tensor'), may hold values from -0.15625 to 0.15625
- w_down: bfloat16 [1472, 3584], P(None, 'tensor'), may hold values from -0.125 to 0.125
- cotangent: bfloat16 [8, 1024, 1472], P(('dp', 'tensor'), 'seq'), may hold values from -6 to 6
Outputs:
- layer_out: float32 [8, 1024, 1472], P(('dp', 'tensor'), 'seq')
- grad_tokens: float32 [8, 1024, 1472], P(('dp', 'tensor'), 'seq')
- grad_gain_attn: float32 [1472], replicated
- grad_w_query: float32 [1472, 384], P('dp', ('tensor', 'seq'))
- grad_w_key: float32 [1472, 384], P('dp', ('tensor', 'seq'))
- grad_w_value: float32 [1472, 384], P('dp', ('tensor', 'seq'))
- grad_w_out: float32 [1472, 384], P('dp', ('tensor', 'seq'))
- grad_rel_table: float32 [32, 6], replicated
- grad_gain_ff: float32 [1472], replicated
- grad_w_gate: float32 [1472, 3584], P('dp', ('tensor', 'seq'))
- grad_w_up: float32 [1472, 3584], P('dp', ('tensor', 'seq'))
- grad_w_down: float32 [1472, 3584], P('dp', ('tensor', 'seq'))
Inputs may be any that keep to these rules, and one draw needn't show every extreme that they name: `segment_ids`: within a row the ids never fall; a document holds 1 to 896 positions, and in every row one holds exactly 896. `buckets`: the bucket depends only on the offset d: it is 0 at d = 0, never falls as |d| grows with d's sign fixed, and is raised by 16 for d > 0.
All inputs are finite; a program needn't handle non-finite values.
Results may differ from a plain program's by a relative error of at most 0.022.
Values may be sent and summed in bfloat16 or wider, within the bound.
A program may use at most 192 MiB of HBM per device.

v0:
```python
import math

import jax
import jax.numpy as jnp
from jax import lax
from jax.sharding import PartitionSpec as P

eps_norm = 1e-06
gelu_scale = math.sqrt(2.0 / math.pi)
masked_score = -1e30
highest = lax.Precision.HIGHEST


def shortened(shard):

    def short(part):
        return part.astype(jnp.bfloat16) if part.dtype == jnp.float32 else part

    return jax.tree.map(short, shard)


def gelu_tanh(values):
    return (
        0.5 * values * (1.0 + jnp.tanh(gelu_scale * (values + 0.044715 * values * values * values)))
    )


def rms_scale(values, gain_vec):
    return (
        values * lax.rsqrt(jnp.mean(values * values, axis=-1, keepdims=True) + eps_norm) * gain_vec
    )


def gated_unit(gate_pre, up_pre):
    return gelu_tanh(gate_pre) * up_pre


def token_sum(left, right):
    left_flat = left.reshape(-1, left.shape[-1])
    right_flat = right.reshape(-1, right.shape[-1])
    return lax.dot_general(
        left_flat, right_flat, (((0,), (0,)), ((), ())), preferred_element_type=jnp.float32
    )


def times_weight_t(values, weight):
    return lax.dot_general(
        values, weight, (((values.ndim - 1,), (1,)), ((), ())), preferred_element_type=jnp.float32
    )


def toeplitz_rows(window, row_count, col_count):
    window_len = window.shape[1]
    turned = jnp.roll(window, -(row_count - 1), axis=1)
    repeated = jnp.tile(turned, (1, row_count))[:, : row_count * (window_len - 1)]
    return repeated.reshape(window.shape[0], row_count, window_len - 1)[:, :, :col_count]


def diagonal_sums(score_block):
    head_count, row_count, col_count = score_block.shape
    flipped = jnp.flip(score_block, axis=1)
    padded = jnp.pad(flipped, ((0, 0), (0, 0), (0, row_count)))
    sheared = padded.reshape(head_count, row_count * (col_count + row_count))
    sheared = sheared[:, : row_count * (col_count + row_count - 1)]
    return jnp.sum(sheared.reshape(head_count, row_count, col_count + row_count - 1), axis=1)


def shards(
    tokens,
    segment_ids,
    buckets,
    gain_attn,
    w_query,
    w_key,
    w_value,
    w_out,
    rel_table,
    gain_ff,
    w_gate,
    w_up,
    w_down,
    cotangent,
):
    rows_dev, pos_dev, width = tokens.shape
    length = pos_dev * lax.axis_size("seq")
    query_start = lax.axis_index("seq") * pos_dev
    num_buckets, heads_dev = rel_table.shape
    inner_dev = w_query.shape[1]
    head_dim = inner_dev // heads_dev
    window_len = length + pos_dev - 1
    window_start = length - pos_dev - query_start
    tokens_f = tokens.astype(jnp.float32)
    normed_attn, norm_attn_back = jax.vjp(rms_scale, tokens_f, gain_attn.astype(jnp.float32))
    normed_attn = normed_attn.astype(jnp.bfloat16)
    w_pair = jnp.stack((w_key, w_value))
    shard_rows = lax.all_gather(normed_attn, "tensor", axis=0, tiled=True)
    queries = jnp.dot(shard_rows, w_query, preferred_element_type=jnp.float32).astype(jnp.bfloat16)
    pairs = jnp.einsum(
        "rcd,sde->rsce", shard_rows, w_pair, preferred_element_type=jnp.float32
    ).astype(jnp.bfloat16)
    attn_rows, queries, pairs = (shard_rows, queries, pairs)
    pairs_all = lax.all_gather(pairs, "seq", axis=2, tiled=True)
    group_rows = attn_rows.shape[0]
    bucket_ids = jnp.arange(num_buckets, dtype=jnp.int32)
    one_hot_all = (buckets[:, None] == bucket_ids[None, :]).astype(jnp.bfloat16)
    per_offset = jnp.dot(one_hot_all, rel_table, preferred_element_type=jnp.float32)
    window = lax.dynamic_slice_in_dim(per_offset, window_start, window_len, 0)
    pos_bias = toeplitz_rows(window.T, pos_dev, length)
    seg_query = lax.dynamic_slice_in_dim(segment_ids, query_start, pos_dev, 1)
    same_doc = seg_query[:, None, :, None] == segment_ids[:, None, None, :]
    query_heads = queries.reshape(group_rows, pos_dev, heads_dev, head_dim)
    key_heads = pairs_all[:, 0].reshape(group_rows, length, heads_dev, head_dim)
    value_heads = pairs_all[:, 1].reshape(group_rows, length, heads_dev, head_dim)

    def score_rows():
        raw_scores = jnp.einsum(
            "rqhd,rkhd->rhqk", query_heads, key_heads, preferred_element_type=jnp.float32
        )
        return jnp.where(same_doc, raw_scores + pos_bias[None], masked_score)

    scores = score_rows()
    row_max = jnp.max(scores, axis=-1, keepdims=True)
    exp_scores = jnp.exp(scores - row_max)
    row_total = jnp.sum(exp_scores, axis=-1, keepdims=True)
    attn_probs = (exp_scores / row_total).astype(jnp.bfloat16)
    log_total = row_max + jnp.log(row_total)
    context = jnp.einsum(
        "rhqk,rkhd->rqhd", attn_probs, value_heads, preferred_element_type=jnp.float32
    )
    context_low = context.reshape(group_rows, pos_dev, inner_dev).astype(jnp.bfloat16)
    attn_branch = lax.psum_scatter(
        times_weight_t(context_low, w_out).astype(jnp.bfloat16),
        "tensor",
        scatter_dimension=0,
        tiled=True,
    ).astype(jnp.float32)
    after_attn = tokens_f + attn_branch
    normed_ff, norm_ff_back = jax.vjp(rms_scale, after_attn, gain_ff.astype(jnp.float32))
    normed_ff = normed_ff.astype(jnp.bfloat16)
    shard_rows = lax.all_gather(normed_ff, "tensor", axis=0, tiled=True)
    gate_pre = jnp.dot(shard_rows, w_gate, preferred_element_type=jnp.float32)
    up_pre = jnp.dot(shard_rows, w_up, preferred_element_type=jnp.float32)
    ff_rows, gate_pre, up_pre = (shard_rows, gate_pre, up_pre)
    hidden, hidden_back = jax.vjp(gated_unit, gate_pre, up_pre)
    hidden_low = hidden.astype(jnp.bfloat16)
    ff_branch = lax.psum_scatter(
        times_weight_t(hidden_low, w_down).astype(jnp.bfloat16),
        "tensor",
        scatter_dimension=0,
        tiled=True,
    ).astype(jnp.float32)
    layer_out = after_attn + ff_branch
    shard_rows = lax.all_gather(cotangent, "tensor", axis=0, tiled=True)
    grad_rows_ff = shard_rows
    grad_hidden = jnp.dot(shard_rows, w_down, preferred_element_type=jnp.float32)
    grad_w_down = token_sum(grad_rows_ff, hidden_low)
    grad_gate, grad_up = hidden_back(grad_hidden)
    grad_gate = grad_gate.astype(jnp.bfloat16)
    grad_up = grad_up.astype(jnp.bfloat16)
    grad_normed_ff = lax.psum_scatter(
        (times_weight_t(grad_gate, w_gate) + times_weight_t(grad_up, w_up)).astype(jnp.bfloat16),
        "tensor",
        scatter_dimension=0,
        tiled=True,
    ).astype(jnp.float32)
    grad_w_gate = token_sum(ff_rows, grad_gate)
    grad_w_up = token_sum(ff_rows, grad_up)
    grad_mid_norm, grad_gain_ff_local = norm_ff_back(grad_normed_ff)
    grad_after_attn = cotangent.astype(jnp.float32) + grad_mid_norm
    grad_branch = grad_after_attn.astype(jnp.bfloat16)
    shard_rows = lax.all_gather(grad_branch, "tensor", axis=0, tiled=True)
    grad_context = jnp.dot(shard_rows, w_out, preferred_element_type=jnp.float32).astype(
        jnp.bfloat16
    )
    grad_w_out = token_sum(shard_rows, context_low)
    probs_again = jnp.exp(score_rows() - log_total)
    grad_ctx_heads = grad_context.reshape(group_rows, pos_dev, heads_dev, head_dim)
    grad_probs = jnp.einsum(
        "rqhd,rkhd->rhqk", grad_ctx_heads, value_heads, preferred_element_type=jnp.float32
    )
    row_delta = jnp.einsum("rqhd,rqhd->rhq", grad_ctx_heads.astype(jnp.float32), context)
    grad_scores = (probs_again * (grad_probs - row_delta[..., None])).astype(jnp.bfloat16)
    probs_low = probs_again.astype(jnp.bfloat16)
    grad_queries = jnp.einsum(
        "rhqk,rkhd->rqhd", grad_scores, key_heads, preferred_element_type=jnp.float32
    )
    grad_queries = grad_queries.reshape(group_rows, pos_dev, inner_dev).astype(jnp.bfloat16)
    grad_key_part = jnp.einsum(
        "rhqk,rqhd->rkhd", grad_scores, query_heads, preferred_element_type=jnp.float32
    )
    grad_value_part = jnp.einsum(
        "rhqk,rqhd->rkhd", probs_low, grad_ctx_heads, preferred_element_type=jnp.float32
    )
    grad_key_part = grad_key_part.reshape(group_rows, length, inner_dev)
    grad_value_part = grad_value_part.reshape(group_rows, length, inner_dev)
    grad_keys, grad_values = (
        lax.psum_scatter(
            grad_key_part.astype(jnp.bfloat16), "seq", scatter_dimension=1, tiled=True
        ).astype(jnp.float32),
        lax.psum_scatter(
            grad_value_part.astype(jnp.bfloat16), "seq", scatter_dimension=1, tiled=True
        ).astype(jnp.float32),
    )
    grad_keys = grad_keys.astype(jnp.bfloat16)
    grad_values = grad_values.astype(jnp.bfloat16)
    table_window = diagonal_sums(jnp.sum(grad_scores.astype(jnp.float32), axis=0))
    window_ids = lax.dynamic_slice_in_dim(buckets, window_start, window_len, 0)
    window_hot = (window_ids[:, None] == bucket_ids[None, :]).astype(jnp.float32)
    grad_table_local = lax.dot_general(
        window_hot,
        table_window,
        (((0,), (1,)), ((), ())),
        precision=highest,
        preferred_element_type=jnp.float32,
    )
    grad_normed_attn = lax.psum_scatter(
        (
            times_weight_t(grad_queries, w_query)
            + times_weight_t(grad_keys, w_key)
            + times_weight_t(grad_values, w_value)
        ).astype(jnp.bfloat16),
        "tensor",
        scatter_dimension=0,
        tiled=True,
    ).astype(jnp.float32)
    grad_w_query = token_sum(attn_rows, grad_queries)
    grad_w_key = token_sum(attn_rows, grad_keys)
    grad_w_value = token_sum(attn_rows, grad_values)
    grad_tokens_norm, grad_gain_attn_local = norm_attn_back(grad_normed_attn)
    grad_tokens = grad_after_attn + grad_tokens_norm
    table_full = jnp.zeros((num_buckets, heads_dev * lax.axis_size("tensor")), jnp.float32)
    table_full = lax.dynamic_update_slice_in_dim(
        table_full, grad_table_local, lax.axis_index("tensor") * heads_dev, 1
    )
    grad_gain_attn, grad_gain_ff, grad_rel_table = lax.psum(
        (grad_gain_attn_local, grad_gain_ff_local, table_full), ("dp", "tensor", "seq")
    )
    weight_grads = (
        grad_w_query,
        grad_w_key,
        grad_w_value,
        grad_w_out,
        grad_w_gate,
        grad_w_up,
        grad_w_down,
    )
    col_counts = [single.shape[1] for single in weight_grads]
    flat_parts = jax.tree.map(
        lambda part: part.astype(jnp.float32),
        lax.psum_scatter(
            shortened(tuple((single.reshape(-1) for single in weight_grads))),
            "dp",
            scatter_dimension=0,
            tiled=True,
        ),
    )
    shaped_parts = tuple((flat_parts[place].reshape(-1, col_counts[place]) for place in range(7)))
    done_q, done_k, done_v, done_o, done_g, done_u, done_d = jax.tree.map(
        lambda part: part.astype(jnp.float32),
        lax.psum_scatter(shortened(shaped_parts), "seq", scatter_dimension=1, tiled=True),
    )
    return (
        layer_out,
        grad_tokens,
        grad_gain_attn,
        done_q,
        done_k,
        done_v,
        done_o,
        grad_rel_table,
        grad_gain_ff,
        done_g,
        done_u,
        done_d,
    )


def solution(mesh):
    return jax.shard_map(
        shards,
        mesh=mesh,
        in_specs=(
            P(("dp", "tensor"), "seq", None),
            P("dp", None),
            P(),
            P(),
            P(None, "tensor"),
            P(None, "tensor"),
            P(None, "tensor"),
            P(None, "tensor"),
            P(None, "tensor"),
            P(),
            P(None, "tensor"),
            P(None, "tensor"),
            P(None, "tensor"),
            P(("dp", "tensor"), "seq", None),
        ),
        out_specs=(
            P(("dp", "tensor"), "seq", None),
            P(("dp", "tensor"), "seq", None),
            P(),
            P("dp", ("tensor", "seq")),
            P("dp", ("tensor", "seq")),
            P("dp", ("tensor", "seq")),
            P("dp", ("tensor", "seq")),
            P(),
            P(),
            P("dp", ("tensor", "seq")),
            P("dp", ("tensor", "seq")),
            P("dp", ("tensor", "seq")),
        ),
        check_vma=False,
    )
```

profile of v0, /device:TPU:0, one launch (start us, length us, event | category | flops | bytes accessed | tf_op | source)
XLA Modules:
  0.0 809.2 jit_solution(9833022236782173717)
XLA Ops:
  9.4 2.3 fusion.44
  11.8 12.5 %all-gather.6.cloned.1.call-done = bf16[2,256,1472]{1,2,0:T(8,128)(2,1)} async-done(((bf16[1,256,1472]{1,2,0:T(8,128)(2,1)}), bf16[2,256,1472]{1,2,0:T(8,128)(2,1)}) %all-gather.6.cloned.1.call-update) | async-done | bytes 1507344 | tf_op jit(solution)/shard_map/all_gather | solution.py:96
  24.3 2.9 fusion.60
  27.9 2.1 tile.4
  30.1 9.1 %tile.10 = f32[3,327424]{1,0:T(4,128)} reshape(f32[3,256,1279]{2,1,0:T(8,128)} %tile.4) | data formatting | bytes 7858176 | tf_op jit(solution)/shard_map/tile | solution.py:55
  39.2 6.3 slice.34
  45.4 10.0 %reshape.190 = f32[3,256,1278]{2,1,0:T(8,128)} reshape(f32[3,327168]{1,0:T(4,128)} %slice.34) | data formatting | bytes 7852032 | tf_op jit(solution)/shard_map/reshape | solution.py:56
  55.4 4.1 slice.35
  61.1 5.2 all-gather.8.cloned.1.call-done
  66.3 1.7 fusion.83
  68.6 2.5 fusion.21
  71.1 1.9 fusion.1
  73.8 3.1 bitcast_convert_fusion.3
  77.6 1.7 convolution_convert_fusion
  80.0 6.8 reduce-scatter.28.cloned.1.call-done
  89.8 9.4 %all-gather.12.cloned.1.call-done = bf16[2,256,1472]{1,2,0:T(8,128)(2,1)} async-done(((bf16[1,256,1472]{1,2,0:T(8,128)(2,1)}), bf16[2,256,1472]{1,2,0:T(8,128)(2,1)}) %all-gather.12.cloned.1.call-update) | async-done | bytes 1507344 | tf_op jit(solution)/shard_map/all_gather | solution.py:153
  99.2 7.8 fusion.3
  107.0 5.1 all-gather.10.cloned.1.call-done
  112.1 6.3 fusion.9
  118.4 10.2 %fusion.18 = (bf16[2,256,1792]{2,1,0:T(8,128)(2,1)S(1)}, bf16[2,256,1792]{2,1,0:T(8,128)(2,1)S(1)}, bf16[2,256,1792]{2,1,0:T(8,128)(2,1)}) fusion(f32[2,256,1792]{2,1,0:T(8,128)S(1)} %copy-done.14, f32[2,256,1792]{2,1,0:T(8,128)S(1)} %fusion.9, bf16[2,256,1472]{1,2,0:T(8,128)(2,1)S(1)} %copy-done.22, bf16[1472,1792]{1,0:T(8,128)(2,1)} %param.24), kind=kOutput, calls=%fused_computation.32 | convolution fusion | flops 2728656896 | bytes 19628032 | tf_op jit(solution)/shard_map/dot_general | solution.py:141
  128.7 3.1 fusion.7
  131.8 4.0 fusion.29
  136.3 9.9 %reduce-scatter.32.cloned.1.call-done = bf16[1,256,1472]{1,2,0:T(8,128)(2,1)} async-done(((bf16[2,256,1472]{1,2,0:T(8,128)(2,1)}), bf16[1,256,1472]{1,2,0:T(8,128)(2,1)}) %reduce-scatter.32.cloned.1.call-update) | async-done | bytes 753680 | tf_op jit(solution)/shard_map/reduce_scatter | solution.py:160
  146.2 2.3 fusion.46
  150.1 11.0 %all-gather.14.cloned.1.call-done = bf16[2,256,1472]{1,2,0:T(8,128)(2,1)} async-done(((bf16[1,256,1472]{1,2,0:T(8,128)(2,1)}), bf16[2,256,1472]{1,2,0:T(8,128)(2,1)}) %all-gather.14.cloned.1.call-update) | async-done | bytes 1507344 | tf_op jit(solution)/shard_map/all_gather | solution.py:171
  161.1 2.0 convolution_convert_fusion.2
  163.2 7.2 convert_reduce_fusion
  170.4 1.9 convolution_convert_fusion.1
  172.4 7.1 bitcast_convert_fusion.2
  179.5 10.7 %convert_element_type.275 = bf16[2637824]{0:T(1024)(128)(2,1)} reshape(bf16[1472,1792]{1,0:T(8,128)(2,1)} %bitcast_convert_fusion.2) | data formatting | bytes 10551296 | tf_op jit(solution)/shard_map/convert_element_type | solution.py:17
  190.2 7.2 bitcast_convert_fusion.1
  197.4 10.7 %convert_element_type.279 = bf16[2637824]{0:T(1024)(128)(2,1)} reshape(bf16[1472,1792]{1,0:T(8,128)(2,1)} %bitcast_convert_fusion.1) | data formatting | bytes 10551296 | tf_op jit(solution)/shard_map/convert_element_type | solution.py:17
  208.2 6.4 fusion.54
  214.8 7.2 fusion
  222.0 10.7 %convert_element_type.284 = bf16[2637824]{0:T(1024)(128)(2,1)} reshape(bf16[1472,1792]{1,0:T(8,128)(2,1)} %fusion) | data formatting | bytes 10551296 | tf_op jit(solution)/shard_map/convert_element_type | solution.py:17
  232.7 3.2 convolution_convert_fusion.4
  237.8 2.7 convert_element_type.258
  240.5 2.0 fusion.39
  243.6 2.7 convert_element_type.270
  246.3 1.6 fusion.37
  249.1 2.7 convert_element_type.262
  251.8 1.6 fusion.38
  253.6 1.7 convert_element_type.266
  258.2 1.7 fusion.32
  260.1 7.0 fusion.33
  268.4 322.7 %all-reduce.12.cloned.1.call-done = (bf16[282624]{0:T(1024)(128)(2,1)}, bf16[282624]{0:T(1024)(128)(2,1)}, bf16[282624]{0:T(1024)(128)(2,1)}, bf16[282624]{0:T(1...) async-done(((bf16[282624]{0:T(1024)(128)(2,1)}, bf16[282624]{0:T(1024)(128)(2,1)}, bf16[282624]{0:T(1024)(128)(2,1)}, ...) | async-done | bytes 18087952
  600.9 2.3 convert_element_type.276
  603.2 2.6 copy.75
  607.3 2.4 convert_element_type.280
  609.6 2.5 copy.77
  613.9 2.4 convert_element_type.285
  616.3 2.5 copy.79
  618.9 24.7 %rev.4 = f32[3,256,1024]{2,1,0:T(8,128)} reverse(f32[3,256,1024]{2,1,0:T(8,128)} %get-tuple-element.73), dimensions={1} | reverse | bytes 6291456 | tf_op jit(solution)/shard_map/jit(_flip)/rev | solution.py:61
  643.6 2.2 pad_bitcast_fusion
  645.8 2.7 copy.81
  648.5 3.1 slice.36
  651.6 9.4 %reshape.193 = f32[3,256,1279]{2,1,0:T(8,128)} reshape(f32[3,327424]{1,0:T(4,128)} %slice.36) | data formatting | bytes 7858176 | tf_op jit(solution)/shard_map/reshape | solution.py:65
  661.0 2.3 reduce_sum.104
  664.0 2.0 fusion.47
  666.0 41.2 %all-reduce.8 = (f32[1472]{0:T(1024)}, f32[32,6]{0,1:T(8,128)}, f32[1472]{0:T(1024)}) all-reduce(f32[1472]{0:T(1024)S(1)} %get-tuple-element.50, f32[32,6]{0,1:T(8,128)S(1)} %dynamic_update_slice.3, f32[1472]{0:T(1024)S(1)} %get-tuple-element.48), channel_id=1, replica_groups=mesh['dp'=4,'tensor'=2,'seq'=4] {'dp','tensor','seq'}, use_global_device_ids=true, to_apply=%region_13.14 | all-reduce | flops 3136 | bytes 25088 | tf_op jit(solution)/shard_map/psum | solution.py:235
  707.3 3.6 fusion.49
  717.4 15.8 %reduce-scatter.48.cloned.1.call-done = bf16[448,368]{1,0:T(8,128)(2,1)} async-done(((bf16[1792,368]{1,0:T(8,128)(2,1)}), bf16[448,368]{1,0:T(8,128)(2,1)}) %reduce-scatter.48.cloned.1.call-update) | async-done | bytes 329744
  735.3 31.1 %reduce-scatter.50.cloned.1.call-done = bf16[448,368]{1,0:T(8,128)(2,1)} async-done(((bf16[1792,368]{1,0:T(8,128)(2,1)}), bf16[448,368]{1,0:T(8,128)(2,1)}) %reduce-scatter.50.cloned.1.call-update) | async-done | bytes 329744
  768.6 31.3 %reduce-scatter.52.cloned.1.call-done = bf16[448,368]{1,0:T(8,128)(2,1)} async-done(((bf16[1792,368]{1,0:T(8,128)(2,1)}), bf16[448,368]{1,0:T(8,128)(2,1)}) %reduce-scatter.52.cloned.1.call-update) | async-done | bytes 329744
  (197 shorter events, 46.5 us)
Async XLA Ops:
  7.2 70.4 %copy-start = (bf16[1472,192]{0,1:T(8,128)(2,1)S(1)}, bf16[1472,192]{0,1:T(8,128)(2,1)}, u32[]{:S(2)}) copy-start(bf16[1472,192]{0,1:T(8,128)(2,1)} %param.21) | copy-start | bytes 1695748
  7.2 17.1 %copy-start.29 = (bf16[1472,192]{0,1:T(8,128)(2,1)S(1)}, bf16[1472,192]{0,1:T(8,128)(2,1)}, u32[]{:S(2)}) copy-start(bf16[1472,192]{0,1:T(8,128)(2,1)} %param.20) | copy-start | bytes 1695748
  7.2 17.1 %copy-start.27 = (bf16[1472,192]{0,1:T(8,128)(2,1)S(1)}, bf16[1472,192]{0,1:T(8,128)(2,1)}, u32[]{:S(2)}) copy-start(bf16[1472,192]{0,1:T(8,128)(2,1)} %param.19) | copy-start | bytes 1695748
  7.2 17.1 %all-gather.6.cloned.1.call-start = ((), (), s32[]{:S(2)}) async-start(), calls=%async_computation.13 | async-start | bytes 2260992 | tf_op jit(solution)/shard_map/all_gather | solution.py:96
  11.7 54.6 %all-gather.8.cloned.1.call-start = ((), (), s32[]{:S(2)}) async-start(), calls=%async_computation.14 | async-start | bytes 1966080 | tf_op jit(solution)/shard_map/all_gather | solution.py:102
  24.3 3.0 copy-start.33
  24.3 3.0 copy-start.35
  27.2 59.5 %reduce-scatter.28.cloned.1.call-start = ((), (), s32[]{:S(2)}) async-start(), calls=%async_computation.15 | async-start | bytes 2260992 | tf_op jit(solution)/shard_map/reduce_scatter | solution.py:131
  55.4 4.1 copy-start.32
  55.4 4.5 copy-start.6
  55.4 4.5 copy-start.19
  66.3 2.4 copy-start.2
  67.9 3.2 copy-start.10
  68.0 5.1 copy-start.17
  71.1 2.6 copy-start.3
  76.9 0.7 copy-start.23
  77.6 2.4 copy-start.34
  77.6 9.2 %copy-start.4 = (bf16[1,256,1472]{1,2,0:T(8,128)(2,1)S(1)}, bf16[1,256,1472]{1,2,0:T(8,128)(2,1)}, u32[]{:S(2)}) copy-start(bf16[1,256,1472]{1,2,0:T(8,128)(2,1)} %param.14) | copy-start | bytes 2260996
  79.4 19.8 %all-gather.12.cloned.1.call-start = ((), (), s32[]{:S(2)}) async-start(), calls=%async_computation.18 | async-start | bytes 2260992 | tf_op jit(solution)/shard_map/all_gather | solution.py:153
  79.9 32.2 %all-gather.10.cloned.1.call-start = ((), (), s32[]{:S(2)}) async-start(), calls=%async_computation.16 | async-start | bytes 2260992 | tf_op jit(solution)/shard_map/all_gather | solution.py:140
  86.8 1.5 copy-start.7
  89.5 56.7 %reduce-scatter.32.cloned.1.call-start = ((), (), s32[]{:S(2)}) async-start(), calls=%async_computation.19 | async-start | bytes 2260992 | tf_op jit(solution)/shard_map/reduce_scatter | solution.py:160
  112.1 6.3 copy-start.14
  112.1 6.3 copy-start.22
  112.1 16.6 %slice-start = ((s8[5275648]{0:T(1024)(128)(4,1)}), s8[4194304]{0:T(1024)(128)(4,1)S(1)}, s32[]{:S(2)}) async-start(s8[5275648]{0:T(1024)(128)(4,1)} %bitcast.165), calls=%async_computation.32 | async-start | bytes 8388608
  112.1 19.7 %slice-start.2 = ((s8[5275648]{0:T(1024)(128)(4,1)}), s8[4194304]{0:T(1024)(128)(4,1)S(1)}, s32[]{:S(2)}) async-start(s8[5275648]{0:T(1024)(128)(4,1)} %bitcast.196), calls=%async_computation.34 | async-start | bytes 8388608
  118.4 10.3 %slice-start.1 = ((s8[5275648]{0:T(1024)(128)(4,1)}), s8[1081344]{0:T(1024)(128)(4,1)S(1)}, s32[]{:S(2)}) async-start(s8[5275648]{0:T(1024)(128)(4,1)} %bitcast.165), calls=%async_computation.33 | async-start | bytes 2162688
  118.4 13.4 %slice-start.3 = ((s8[5275648]{0:T(1024)(128)(4,1)}), s8[1081344]{0:T(1024)(128)(4,1)S(1)}, s32[]{:S(2)}) async-start(s8[5275648]{0:T(1024)(128)(4,1)} %bitcast.196), calls=%async_computation.35 | async-start | bytes 2162688
  128.7 3.1 copy-start.37
  128.7 3.1 copy-start.38
  135.9 25.2 %all-gather.14.cloned.1.call-start = ((), (), s32[]{:S(2)}) async-start(), calls=%async_computation.20 | async-start | bytes 2260992 | tf_op jit(solution)/shard_map/all_gather | solution.py:171
  146.2 2.3 copy-start.8
  146.2 2.3 copy-start.11
  146.2 2.3 copy-start.13
  150.1 96.3 %reduce-scatter.34.cloned.1.call-start = ((), (), s32[]{:S(2)}) async-start(), calls=%async_computation.21 | async-start | bytes 983040 | tf_op jit(solution)/shard_map/reduce_scatter | solution.py:197
  161.1 2.0 copy-start.31
  161.1 2.1 copy-start.18
  163.1 7.3 copy-start.15
  163.2 7.2 copy-start.21
  170.4 1.9 copy-start.5
  172.3 79.4 %reduce-scatter.36.cloned.1.call-start = ((), (), s32[]{:S(2)}) async-start(), calls=%async_computation.22 | async-start | bytes 983040 | tf_op jit(solution)/shard_map/reduce_scatter | solution.py:200
  197.4 10.8 %copy-start.16 = (bf16[2,256,192]{1,2,0:T(8,128)(2,1)S(1)}, bf16[2,256,192]{1,2,0:T(8,128)(2,1)}, u32[]{:S(2)}) copy-start(bf16[2,256,192]{1,2,0:T(8,128)(2,1)} %copy-done.15) | copy-start | bytes 589828
  214.6 376.5 %all-reduce.12.cloned.1.call-start = ((), (), s32[]{:S(2)}) async-start(), calls=%async_computation.31 | async-start | bytes 36175872
  236.6 3.9 copy-start.24
  255.3 1.1 copy-start.20
  255.4 1.7 copy-start.25
  255.4 1.7 copy-start.28
  255.4 408.6 %reduce-scatter.38.cloned.1.call-start = ((), (), s32[]{:S(2)}) async-start(), calls=%async_computation.23 | async-start | bytes 2260992 | tf_op jit(solution)/shard_map/reduce_scatter | solution.py:216
  257.0 0.9 copy-start.26
  257.0 1.2 copy-start.30
  258.2 1.8 copy-start.39
  260.0 7.2 copy-start.36
  260.0 447.2 %reduce-scatter.30.cloned.1.call-start = ((), (), s32[]{:S(2)}) async-start(), calls=%async_computation.17 | async-start | bytes 2260992 | tf_op jit(solution)/shard_map/reduce_scatter | solution.py:146
  267.1 443.8 %reduce-scatter.40.cloned.1.call-start = ((), (), s32[]{:S(2)}) async-start(), calls=%async_computation.24 | async-start | bytes 184320
  593.0 119.6 %reduce-scatter.42.cloned.1.call-start = ((), (), s32[]{:S(2)}) async-start(), calls=%async_computation.25 | async-start | bytes 184320
  594.9 119.2 %reduce-scatter.44.cloned.1.call-start = ((), (), s32[]{:S(2)}) async-start(), calls=%async_computation.26 | async-start | bytes 184320
  596.8 118.9 %reduce-scatter.46.cloned.1.call-start = ((), (), s32[]{:S(2)}) async-start(), calls=%async_computation.27 | async-start | bytes 184320
  598.8 134.4 %reduce-scatter.48.cloned.1.call-start = ((), (), s32[]{:S(2)}) async-start(), calls=%async_computation.28 | async-start | bytes 1720320
  605.8 160.6 %reduce-scatter.50.cloned.1.call-start = ((), (), s32[]{:S(2)}) async-start(), calls=%async_computation.29 | async-start | bytes 1720320
  612.2 187.8 %reduce-scatter.52.cloned.1.call-start = ((), (), s32[]{:S(2)}) async-start(), calls=%async_computation.30 | async-start | bytes 1720320
  663.4 43.9 %copy-start.9 = (bf16[1,256,1472]{1,2,0:T(8,128)(2,1)S(1)}, bf16[1,256,1472]{1,2,0:T(8,128)(2,1)}, u32[]{:S(2)}) copy-start(bf16[1,256,1472]{1,2,0:T(8,128)(2,1)} %reduce-scatter.28.cloned.1.call-done) | copy-start | bytes 2260996
  663.4 43.9 %copy-start.12 = (bf16[1,256,1472]{1,2,0:T(8,128)(2,1)S(1)}, bf16[1,256,1472]{1,2,0:T(8,128)(2,1)}, u32[]{:S(2)}) copy-start(bf16[1,256,1472]{1,2,0:T(8,128)(2,1)} %param.27) | copy-start | bytes 2260996
  734.3 67.8 %copy-start.1 = (bf16[1472,192]{0,1:T(8,128)(2,1)S(1)}, bf16[1472,192]{0,1:T(8,128)(2,1)}, u32[]{:S(2)}) copy-start(bf16[1472,192]{0,1:T(8,128)(2,1)} %param.21) | copy-start | bytes 1695748
Sparse Core Ops, SparseCore 0:
  11.8 12.3 all-gather.5
  27.4 38.8 all-gather.7
  79.5 7.2 reduce-scatter.27
  88.2 10.8 all-gather.11
  101.2 10.8 all-gather.9
  136.0 10.1 reduce-scatter.31
  150.2 10.9 all-gather.13
  172.5 24.4 reduce-scatter.33
  214.7 24.4 reduce-scatter.35
  255.5 335.5 all-reduce.11
  594.0 10.0 reduce-scatter.37
  606.7 10.2 reduce-scatter.29
  619.9 20.4 reduce-scatter.39
  643.1 17.4 reduce-scatter.41
  663.4 17.4 reduce-scatter.43
  683.0 17.5 reduce-scatter.45
  702.8 30.2 reduce-scatter.47
  735.3 31.0 reduce-scatter.49
  768.8 31.0 reduce-scatter.51
where the time goes:
time: 818 us; the launch traced here: 809 us
  waiting for transfers between devices  462 us (56%)
  local copies, waits for them, and re-layouts  165 us (20%)
  matrix products  102 us (12%)
  blocking collectives  41.2 us (5%)
  other arithmetic  21.2 us (3%)
  between operations  16.5 us (2%)
    unnamed x27, waiting for transfers between devices  402 us
    convert_element_type x18, local copies, waits for them, and re-layouts, short(): return part.astype(jnp.bfloat16) if part.dtype == jnp.float32 else part  53.3 us
    psum x1, blocking collectives, shards(): lax.psum((grad_gain_attn_local, grad_gain_ff_local, table_full), ('dp', '...  41.2 us
    unnamed x119, local copies, waits for them, and re-layouts  40.7 us
    dot_general x7, matrix products, token_sum(): lax.dot_general(left_flat, right_flat, (((0,), (0,)), ((), ())), preferre...  27.3 us
    rev x1, local copies, waits for them, and re-layouts, diagonal_sums(): flipped = jnp.flip(score_block, axis=1)  24.7 us
    dot_general x7, matrix products, times_weight_t(): lax.dot_general(values, weight, (((values.ndim - 1,), (1,)), ((), ())), p...  18.9 us
  transfers between devices with their start and end apart: 19, of which 11 were waited for; matrix products, arithmetic and copies ran while one was open for 27% of the time, Pallas kernels for 0%

commit v1 on v0

--- a/solution.py
+++ b/solution.py
@@ -3,6 +3,8 @@
 import jax
 import jax.numpy as jnp
 from jax import lax
+from jax.experimental import pallas as pl
+from jax.experimental.pallas import tpu as pltpu
 from jax.sharding import PartitionSpec as P
 
 eps_norm = 1e-06
@@ -63,6 +65,275 @@
     sheared = padded.reshape(head_count, row_count * (col_count + row_count))
     sheared = sheared[:, : row_count * (col_count + row_count - 1)]
     return jnp.sum(sheared.reshape(head_count, row_count, col_count + row_count - 1), axis=1)
+
+
+f32, bf16 = jnp.float32, jnp.bfloat16
+MESH = pl.DeviceIdType.MESH
+NT = (((1,), (1,)), ((), ()))
+TN = (((0,), (0,)), ((), ()))
+
+
+def dot_f32(left, right, dims=(((1,), (0,)), ((), ()))):
+    return lax.dot_general(left, right, dims, preferred_element_type=f32)
+
+
+class Links:
+    def __init__(self, send_sems, recv_sems):
+        self.send_sems, self.recv_sems, self.count, self.open = send_sems, recv_sems, 0, []
+        dp, core, seq = lax.axis_index("dp"), lax.axis_index("tensor"), lax.axis_index("seq")
+        self.dp, self.t, self.s = dp, core, seq
+        self.x = lax.rem(dp, 2)
+        self.y = lax.div(dp, 2)
+        self.core = (dp, 1 - core, seq)
+        self.xdev = (dp + 1 - 2 * self.x, core, seq)
+        self.ydev = (dp + 2 - 4 * self.y, core, seq)
+
+    def z(self, step):
+        return (self.dp, self.t, lax.rem(self.s + step + 4, 4))
+
+    def to_seq(self, target):
+        return (self.dp, self.t, target)
+
+    def slots(self, amount=1):
+        first = self.count
+        self.count += amount
+        return first
+
+    def copy(self, src, dst, device, slot=None):
+        slot = self.slots() if slot is None else slot
+        return pltpu.make_async_remote_copy(
+            src_ref=src,
+            dst_ref=dst,
+            send_sem=self.send_sems.at[slot],
+            recv_sem=self.recv_sems.at[slot],
+            device_id=device,
+            device_id_type=MESH,
+        )
+
+    def send(self, src, dst, device):
+        single = self.copy(src, dst, device)
+        single.start()
+        self.open.append(single)
+        return single
+
+    def finish(self):
+        for single in self.open:
+            single.wait_send()
+        self.open = []
+
+    def greet(self, devices):
+        barrier = pltpu.get_barrier_semaphore()
+        for device in devices:
+            pl.semaphore_signal(barrier, inc=1, device_id=device, device_id_type=MESH)
+        pl.semaphore_wait(barrier, len(devices))
+
+
+def unit_scale(values):
+    return lax.rsqrt(jnp.mean(values * values, axis=-1, keepdims=True) + eps_norm)
+
+
+def forward_kernel(
+    tokens,
+    cotangent,
+    seg_rows,
+    bucket_window,
+    table_t,
+    gain_attn,
+    gain_ff,
+    w_query,
+    w_key,
+    w_value,
+    w_out,
+    normed_pair,
+    queries,
+    pairs,
+    context,
+    log_total,
+    after_attn,
+    ff_pair,
+    cot_pair,
+    cot_near,
+    bias,
+    per_offset,
+    send_buf,
+    recv_buf,
+    local_sem,
+    send_sems,
+    recv_sems,
+):
+    links = Links(send_sems, recv_sems)
+    t, s = links.t, links.s
+    rows, pos, width = normed_pair.shape
+    inner = queries.shape[2]
+    heads = bias.shape[0]
+    dh = inner // heads
+    links.greet([links.core, links.xdev, links.z(1), links.z(2), links.z(3)])
+    own_cot = pltpu.make_async_copy(cotangent, cot_pair.at[t], local_sem)
+    own_cot.start()
+    cot_core = links.send(cotangent, cot_pair.at[t], links.core)
+    cot_x = links.send(cotangent, cot_near.at[t], links.xdev)
+
+    values = tokens[...].astype(f32)
+    normed_pair[t] = (values * unit_scale(values) * gain_attn[...]).astype(bf16)
+    normed_core = links.send(normed_pair.at[t], normed_pair.at[t], links.core)
+
+    chain = links.slots(2 * 3 * 2)
+
+    def hop(way, step, row):
+        slot = chain + (way * 3 + step - 1) * 2 + row
+        step_by = 1 if way == 0 else -1
+        block = lax.rem(s - step_by * (step - 1) + 4, 4)
+        place = lax.rem(t + row, 2)
+        return links.copy(
+            pairs.at[block, place], pairs.at[block, place], links.z(step_by), slot
+        )
+
+    def sends(way, step):
+        return (s >= step - 1) & (s < 3) if way == 0 else (s <= 4 - step) & (s > 0)
+
+    def receives(way, step):
+        return s >= step if way == 0 else s <= 3 - step
+
+    def project(place, row):
+        block = normed_pair[place]
+        queries[place] = dot_f32(block, w_query[...]).astype(bf16)
+        pairs[s, place] = jnp.concatenate(
+            [dot_f32(block, w_key[...]), dot_f32(block, w_value[...])], axis=1
+        ).astype(bf16)
+        for way in range(2):
+            pl.when(sends(way, 1))(lambda way=way: hop(way, 1, row).start())
+
+    project(t, 0)
+    normed_core.wait_recv()
+    project(1 - t, 1)
+
+    bucket_ids = lax.broadcasted_iota(jnp.int32, (table_t.shape[1], bucket_window.shape[1]), 0)
+    one_hot = (bucket_ids == bucket_window[...]).astype(bf16)
+    per_offset[...] = dot_f32(table_t[...], one_hot)
+    window = per_offset[:, pl.ds(pl.multiple_of(s * pos, 128), 5 * pos)]
+    for head in range(heads):
+        for block in range(4):
+            strip = jnp.concatenate(
+                [
+                    window[head : head + 1, (4 - block) * pos : (5 - block) * pos],
+                    window[head : head + 1, (3 - block) * pos : (4 - block) * pos],
+                ],
+                axis=1,
+            )
+            strip = jnp.broadcast_to(strip, (pos, 2 * pos))
+            strip = pltpu.roll(strip, 1, 1, stride=1, stride_axis=0)
+            bias[head, block] = strip[:, :pos].astype(bf16)
+
+    for step in (1, 2):
+        for row in range(2):
+            for way in range(2):
+                pl.when(receives(way, step))(
+                    lambda way=way, step=step, row=row: hop(way, step, row).wait_recv()
+                )
+                pl.when(sends(way, step + 1))(
+                    lambda way=way, step=step, row=row: hop(way, step + 1, row).start()
+                )
+    cot_x.wait_recv()
+    cot_far = links.send(cot_near.at[t], cot_near.at[t], links.core)
+    for row in range(2):
+        for way in range(2):
+            pl.when(receives(way, 3))(lambda way=way, row=row: hop(way, 3, row).wait_recv())
+
+    def attend(row, carry):
+        seg_query = seg_rows[row, :, pl.ds(pl.multiple_of(s * pos, 128), pos)]
+        same = []
+        for block in range(4):
+            seg_key = seg_rows[row, :, block * pos : (block + 1) * pos]
+            same.append(jnp.broadcast_to(seg_key, (pos, pos)).T == seg_query)
+        parts = []
+        for head in range(heads):
+            lanes = slice(head * dh, (head + 1) * dh)
+            lanes_v = slice(inner + head * dh, inner + (head + 1) * dh)
+            query = queries[row, :, lanes]
+            scores = [
+                jnp.where(
+                    same[block],
+                    dot_f32(pairs[block, row, :, lanes], query, NT) + bias[head, block].astype(f32),
+                    masked_score,
+                )
+                for block in range(4)
+            ]
+            top = jnp.max(scores[0], axis=0, keepdims=True)
+            for block in range(1, 4):
+                top = jnp.maximum(top, jnp.max(scores[block], axis=0, keepdims=True))
+            total = jnp.zeros_like(top)
+            mixed = jnp.zeros((dh, pos), f32)
+            for block in range(4):
+                grown = jnp.exp(scores[block] - top)
+                total = total + jnp.sum(grown, axis=0, keepdims=True)
+                mixed = mixed + dot_f32(pairs[block, row, :, lanes_v], grown.astype(bf16), TN)
+            log_total[row, head : head + 1] = top + jnp.log(total)
+            parts.append(mixed * (1.0 / total))
+        context[row] = jnp.concatenate(parts, axis=0).T.astype(bf16)
+        return carry
+
+    lax.fori_loop(0, rows, attend, 0)
+
+    send_buf[...] = dot_f32(context[1 - t], w_out[...], NT).astype(bf16)
+    branch_core = links.send(send_buf, recv_buf, links.core)
+    branch = dot_f32(context[t], w_out[...], NT)
+    branch_core.wait_recv()
+    values = tokens[...].astype(f32) + (branch + recv_buf[...].astype(f32))
+    after_attn[...] = values
+    ff_pair[t] = (values * unit_scale(values) * gain_ff[...]).astype(bf16)
+    ff_core = links.send(ff_pair.at[t], ff_pair.at[t], links.core)
+    ff_core.wait_recv()
+    cot_core.wait_recv()
+    cot_far.wait_recv()
+    own_cot.wait()
+    links.finish()
+    for step in (1, 2, 3):
+        for row in range(2):
+            for way in range(2):
+                pl.when(sends(way, step))(
+                    lambda way=way, step=step, row=row: hop(way, step, row).wait_send()
+                )
+
+
+def vmem_spec():
+    return pl.BlockSpec(memory_space=pltpu.VMEM)
+
+
+def forward_part(tokens, cotangent, seg_rows, bucket_window, table_t, gain_attn, gain_ff, w_query, w_key, w_value, w_out):
+    pos, width = tokens.shape
+    inner = w_query.shape[1]
+    heads = 3
+    shape = jax.ShapeDtypeStruct
+    outs = (
+        shape((2, pos, width), bf16),
+        shape((2, pos, inner), bf16),
+        shape((4, 2, pos, 2 * inner), bf16),
+        shape((2, pos, inner), bf16),
+        shape((2, heads, pos), f32),
+        shape((pos, width), f32),
+        shape((2, pos, width), bf16),
+        shape((2, pos, width), bf16),
+        shape((2, pos, width), bf16),
+        shape((heads, 4, pos, pos), bf16),
+    )
+    return pl.pallas_call(
+        forward_kernel,
+        out_shape=outs,
+        in_specs=[vmem_spec()] * 11,
+        out_specs=tuple(vmem_spec() for _ in outs),
+        scratch_shapes=[
+            pltpu.VMEM((8, 2048), f32),
+            pltpu.VMEM((pos, width), bf16),
+            pltpu.VMEM((pos, width), bf16),
+            pltpu.SemaphoreType.DMA,
+            pltpu.SemaphoreType.DMA((20,)),
+            pltpu.SemaphoreType.DMA((20,)),
+        ],
+        compiler_params=pltpu.CompilerParams(
+            collective_id=1, has_side_effects=True, vmem_limit_bytes=56 * 2**20
+        ),
+        name="forward_part",
+    )(tokens, cotangent, seg_rows, bucket_window, table_t, gain_attn, gain_ff, w_query, w_key, w_value, w_out)
 
 
 def shards(
@@ -91,53 +362,31 @@
     window_start = length - pos_dev - query_start
     tokens_f = tokens.astype(jnp.float32)
     normed_attn, norm_attn_back = jax.vjp(rms_scale, tokens_f, gain_attn.astype(jnp.float32))
-    normed_attn = normed_attn.astype(jnp.bfloat16)
-    w_pair = jnp.stack((w_key, w_value))
-    shard_rows = lax.all_gather(normed_attn, "tensor", axis=0, tiled=True)
-    queries = jnp.dot(shard_rows, w_query, preferred_element_type=jnp.float32).astype(jnp.bfloat16)
-    pairs = jnp.einsum(
-        "rcd,sde->rsce", shard_rows, w_pair, preferred_element_type=jnp.float32
-    ).astype(jnp.bfloat16)
-    attn_rows, queries, pairs = (shard_rows, queries, pairs)
-    pairs_all = lax.all_gather(pairs, "seq", axis=2, tiled=True)
-    group_rows = attn_rows.shape[0]
+    bwin = jnp.pad(jnp.flip(buckets), (0, 1))[None]
+    table_t = jnp.pad(rel_table.T, ((0, 5), (0, 0)))
+    attn_rows, queries, kv_all, context_low, lse, aa, ff_rows0, grad_rows_ff, cot_near, biasT = forward_part(
+        tokens[0], cotangent[0], segment_ids[:, None, :], bwin, table_t, gain_attn.astype(jnp.float32)[None], gain_ff.astype(jnp.float32)[None], w_query, w_key, w_value, w_out)
+    group_rows = 2
     bucket_ids = jnp.arange(num_buckets, dtype=jnp.int32)
-    one_hot_all = (buckets[:, None] == bucket_ids[None, :]).astype(jnp.bfloat16)
-    per_offset = jnp.dot(one_hot_all, rel_table, preferred_element_type=jnp.float32)
-    window = lax.dynamic_slice_in_dim(per_offset, window_start, window_len, 0)
-    pos_bias = toeplitz_rows(window.T, pos_dev, length)
-    seg_query = lax.dynamic_slice_in_dim(segment_ids, query_start, pos_dev, 1)
-    same_doc = seg_query[:, None, :, None] == segment_ids[:, None, None, :]
+    log_total = lse[..., None]
+    context = context_low.astype(jnp.float32).reshape(2, pos_dev, heads_dev, head_dim)
+    kvt = kv_all.transpose(1, 0, 2, 3).reshape(2, length, 384)
+    pairs_all = jnp.stack([kvt[..., :192], kvt[..., 192:]], 1)
     query_heads = queries.reshape(group_rows, pos_dev, heads_dev, head_dim)
     key_heads = pairs_all[:, 0].reshape(group_rows, length, heads_dev, head_dim)
     value_heads = pairs_all[:, 1].reshape(group_rows, length, heads_dev, head_dim)
+    pos_bias = biasT.reshape(3, length, pos_dev).transpose(0, 2, 1).astype(jnp.float32)
+    seg_query = lax.dynamic_slice_in_dim(segment_ids, query_start, pos_dev, 1)
+    same_doc = seg_query[:, None, :, None] == segment_ids[:, None, None, :]
 
     def score_rows():
         raw_scores = jnp.einsum(
             "rqhd,rkhd->rhqk", query_heads, key_heads, preferred_element_type=jnp.float32
         )
         return jnp.where(same_doc, raw_scores + pos_bias[None], masked_score)
-
-    scores = score_rows()
-    row_max = jnp.max(scores, axis=-1, keepdims=True)
-    exp_scores = jnp.exp(scores - row_max)
-    row_total = jnp.sum(exp_scores, axis=-1, keepdims=True)
-    attn_probs = (exp_scores / row_total).astype(jnp.bfloat16)
-    log_total = row_max + jnp.log(row_total)
-    context = jnp.einsum(
-        "rhqk,rkhd->rqhd", attn_probs, value_heads, preferred_element_type=jnp.float32
-    )
-    context_low = context.reshape(group_rows, pos_dev, inner_dev).astype(jnp.bfloat16)
-    attn_branch = lax.psum_scatter(
-        times_weight_t(context_low, w_out).astype(jnp.bfloat16),
-        "tensor",
-        scatter_dimension=0,
-        tiled=True,
-    ).astype(jnp.float32)
-    after_attn = tokens_f + attn_branch
+    after_attn = aa[None]
     normed_ff, norm_ff_back = jax.vjp(rms_scale, after_attn, gain_ff.astype(jnp.float32))
-    normed_ff = normed_ff.astype(jnp.bfloat16)
-    shard_rows = lax.all_gather(normed_ff, "tensor", axis=0, tiled=True)
+    shard_rows = ff_rows0
     gate_pre = jnp.dot(shard_rows, w_gate, preferred_element_type=jnp.float32)
     up_pre = jnp.dot(shard_rows, w_up, preferred_element_type=jnp.float32)
     ff_rows, gate_pre, up_pre = (shard_rows, gate_pre, up_pre)
@@ -150,8 +399,7 @@
         tiled=True,
     ).astype(jnp.float32)
     layer_out = after_attn + ff_branch
-    shard_rows = lax.all_gather(cotangent, "tensor", axis=0, tiled=True)
-    grad_rows_ff = shard_rows
+    shard_rows = grad_rows_ff
     grad_hidden = jnp.dot(shard_rows, w_down, preferred_element_type=jnp.float32)
     grad_w_down = token_sum(grad_rows_ff, hidden_low)
     grad_gate, grad_up = hidden_back(grad_hidden)

time: 818 us -> 771 us (0.943)
  waiting for transfers between devices: 462 us -> 403 us
  Pallas kernels: 0 us -> 49 us
  matrix products: 102 us -> 85.5 us
  local copies, waits for them, and re-layouts: 165 us -> 149 us
    pallas_call x0 -> x1, Pallas kernels: none -> 49 us  [forward_part(): pl.pallas_call(forward_kernel, out_shape=outs, in_specs=[vmem_spec()] * 1...]
    all_gather x4 -> x0, waiting for transfers between devices: 32.2 us -> none  [the longest x1 12.5 us: shards(): shard_rows = lax.all_gather(normed_attn, 'tensor', axis=0, tiled=True)]
    another operation x2 -> x0, local copies, waits for them, and re-layouts: 11.2 us -> none  [toeplitz_rows(): jnp.tile(turned, (1, row_count))[:, :row_count * (window_len - 1)]]
    all_gather x1, waiting for transfers between devices: 11 us -> 0.01 us  [shards(): shard_rows = lax.all_gather(grad_branch, 'tensor', axis=0, tiled=True)]
    reshape x1 -> x0, local copies, waits for them, and re-layouts: 9.97 us -> none  [toeplitz_rows(): repeated.reshape(window.shape[0], row_count, window_len - 1)]
    unnamed x119 -> x140, local copies, waits for them, and re-layouts: 40.7 us -> 50 us
    slice x5 -> x3, local copies, waits for them, and re-layouts: 12.1 us -> 3.37 us  [shards(): pairs_all = jnp.stack([kvt[..., :192], kvt[..., 192:]], 1)]
    unnamed x27 -> x22, waiting for transfers between devices: 402 us -> 394 us
  transfers between devices with their start and end apart: 19 -> 14, of which waited for: 11 -> 5; matrix products, arithmetic and copies ran while one was open for 27% -> 25% of each run, Pallas kernels for 0% -> 0%
where the time goes in v1:
time: 771 us; the launch traced here: 760 us
  waiting for transfers between devices  403 us (52%)
  local copies, waits for them, and re-layouts  149 us (19%)
  matrix products  85.5 us (11%)
  Pallas kernels  49 us (6%)
  blocking collectives  40.9 us (5%)
  between operations  16.3 us (2%)
  other arithmetic  14.8 us (2%)
    unnamed x22, waiting for transfers between devices  394 us
    unnamed x140, local copies, waits for them, and re-layouts  50 us
    pallas_call x1, Pallas kernels, forward_part(): pl.pallas_call(forward_kernel, out_shape=outs, in_specs=[vmem_spec()] * 1...  49 us
    convert_element_type x18, local copies, waits for them, and re-layouts, short(): return part.astype(jnp.bfloat16) if part.dtype == jnp.float32 else part  45.7 us
    psum x1, blocking collectives, shards(): lax.psum((grad_gain_attn_local, grad_gain_ff_local, table_full), ('dp', '...  40.9 us
    dot_general x7, matrix products, token_sum(): lax.dot_general(left_flat, right_flat, (((0,), (0,)), ((), ())), preferre...  26.6 us
    rev x1, local copies, waits for them, and re-layouts, diagonal_sums(): flipped = jnp.flip(score_block, axis=1)  24.7 us
    dot_general x6, matrix products, times_weight_t(): lax.dot_general(values, weight, (((values.ndim - 1,), (1,)), ((), ())), p...  17.9 us
  transfers between devices with their start and end apart: 14, of which 5 were waited for; matrix products, arithmetic and copies ran while one was open for 25% of the time, Pallas kernels for 0%

profile of v1, /device:TPU:0, one launch (start us, length us, event | category | flops | bytes accessed | tf_op | source)
XLA Modules:
  0.0 759.7 jit_solution(13326887752604187359)
XLA Ops:
  7.3 2.4 copy.190
  15.1 1.2 copy.194.w_value
  18.6 49.0 %forward_part.1 = (bf16[2,256,1472]{2,1,0:T(8,128)(2,1)}, bf16[2,256,192]{2,1,0:T(8,128)(2,1)}, bf16[4,2,256,384]{3,2,1,0:T(8,128)(2,1)}, bf16[2,256,192]{2,1,0:...) custom-call(bf16[256,1472]{1,0:T(8,128)(2,1)} %bitcast.150, ...), custom_call_target="tpu_custom_call" | custom-call | tf_op jit(solution)/shard_map/forward_part/pallas_call | solution.py:319
  67.7 6.1 fusion
  73.9 3.0 fusion.6
  76.9 8.0 %fusion.16 = (bf16[2,256,1792]{2,1,0:T(8,128)(2,1)S(1)}, bf16[2,256,1792]{2,1,0:T(8,128)(2,1)S(1)}, bf16[2,256,1792]{2,1,0:T(8,128)(2,1)}) fusion(f32[2,256,1792]{2,1,0:T(8,128)S(1)} %fusion, f32[2,256,1792]{2,1,0:T(8,128)S(1)} %fusion.6, bf16[2,256,1472]{2,1,0:T(8,128)(2,1)S(1)} %copy-done.41, bf16[1472,1792]{1,0:T(8,128)(2,1)S(1)} %bitcast.187), kind=kOutput, calls=%fused_computation.27 | convolution fusion | flops 2728656896 | bytes 19628032 | tf_op jit(solution)/shard_map/dot_general | solution.py:390
  85.0 2.9 fusion.4
  87.9 3.0 fusion.19
  91.0 1.6 copy.201
  92.9 8.0 %reduce-scatter.29.cloned.1.call-done = bf16[1,256,1472]{2,1,0:T(8,128)(2,1)} async-done(((bf16[2,256,1472]{2,1,0:T(8,128)(2,1)}), bf16[1,256,1472]{2,1,0:T(8,128)(2,1)}) %reduce-scatter.29.cloned.1.call-update) | async-done | bytes 753680 | tf_op jit(solution)/shard_map/reduce_scatter | solution.py:408
  100.9 2.3 fusion.37
  106.2 1.6 copy.203
  108.6 1.2 copy.207
  110.0 2.0 convert_bitcast_fusion
  112.0 2.6 copy.205
  114.7 1.2 broadcast_compare_fusion
  115.9 4.8 fusion.59
  120.7 2.2 convolution_convert_fusion.1
  123.0 6.7 convert_reduce_fusion
  129.7 1.9 convolution_convert_fusion
  131.7 7.2 bitcast_convert_fusion.2
  138.9 10.8 %convert_element_type.248 = bf16[2637824]{0:T(1024)(128)(2,1)} reshape(bf16[1472,1792]{1,0:T(8,128)(2,1)} %bitcast_convert_fusion.2) | data formatting | bytes 10551296 | tf_op jit(solution)/shard_map/convert_element_type | solution.py:19
  149.7 7.3 bitcast_convert_fusion.1
  157.0 10.7 %convert_element_type.252 = bf16[2637824]{0:T(1024)(128)(2,1)} reshape(bf16[1472,1792]{1,0:T(8,128)(2,1)} %bitcast_convert_fusion.1) | data formatting | bytes 10551296 | tf_op jit(solution)/shard_map/convert_element_type | solution.py:19
  167.7 5.6 fusion.43
  173.3 7.3 bitcast_convert_fusion
  180.6 11.1 %convert_element_type.256 = bf16[2637824]{0:T(1024)(128)(2,1)} reshape(bf16[1472,1792]{1,0:T(8,128)(2,1)} %bitcast_convert_fusion) | data formatting | bytes 10551296 | tf_op jit(solution)/shard_map/convert_element_type | solution.py:19
  191.7 2.3 convolution_convert_fusion.2
  194.8 1.7 convert_element_type.231
  196.5 1.6 fusion.29
  198.3 1.7 convert_element_type.243
  200.1 1.4 fusion.31
  201.8 1.7 convert_element_type.235
  203.5 1.4 fusion.32
  205.2 1.7 convert_element_type.239
  208.6 2.2 convolution_add_fusion
  210.8 2.4 copy.209
  213.2 3.0 fusion.25
  216.7 6.0 fusion.26
  222.8 1.6 copy.198
  225.7 317.0 %all-reduce.14.cloned.1.call-done = (bf16[282624]{0:T(1024)(128)(2,1)}, bf16[282624]{0:T(1024)(128)(2,1)}, bf16[282624]{0:T(1024)(128)(2,1)}, bf16[282624]{0:T(1...) async-done(((bf16[282624]{0:T(1024)(128)(2,1)}, bf16[282624]{0:T(1024)(128)(2,1)}, bf16[282624]{0:T(1024)(128)(2,1)}, ...) | async-done | bytes 18087952
  551.1 1.7 dynamic-slice.9
  552.8 1.5 convert_element_type.249
  554.3 1.6 copy.259
  555.9 1.4 dynamic-slice.11
  557.3 1.5 convert_element_type.253
  558.9 1.6 copy.261
  560.7 1.4 dynamic-slice.13
  562.1 1.5 convert_element_type.257
  563.7 1.5 copy.263
  565.6 24.7 %rev.9 = f32[3,256,1024]{2,1,0:T(8,128)} reverse(f32[3,256,1024]{2,1,0:T(8,128)} %get-tuple-element.111), dimensions={1} | reverse | bytes 6291456 | tf_op jit(solution)/shard_map/jit(_flip)/rev | solution.py:63
  590.3 2.2 pad_bitcast_fusion
  592.6 2.7 copy.265
  595.3 3.1 slice.14
  598.4 9.5 %reshape.187 = f32[3,256,1279]{2,1,0:T(8,128)} reshape(f32[3,327424]{1,0:T(4,128)} %slice.14) | data formatting | bytes 7858176 | tf_op jit(solution)/shard_map/reshape | solution.py:67
  607.8 2.4 reduce_sum.79
  611.0 1.8 fusion.38
  613.0 4.1 fusion.40
  617.0 3.1 copy.223
  620.2 1.6 copy.224
  621.7 40.9 %all-reduce.10 = (f32[1472]{0:T(1024)}, f32[32,6]{0,1:T(8,128)}, f32[1472]{0:T(1024)}) all-reduce(f32[1472]{0:T(1024)S(1)} %get-tuple-element.92, f32[32,6]{0,1:T(8,128)S(1)} %dynamic_update_slice.3, f32[1472]{0:T(1024)S(1)} %copy-done.30), channel_id=1, replica_groups=mesh['dp'=4,'tensor'=2,'seq'=4] {'dp','tensor','seq'}, use_global_device_ids=true, to_apply=%region_10.11 | all-reduce | flops 3136 | bytes 25088 | tf_op jit(solution)/shard_map/psum | solution.py:483
  669.1 14.8 %reduce-scatter.45.cloned.1.call-done = bf16[448,368]{1,0:T(8,128)(2,1)} async-done(((bf16[1792,368]{1,0:T(8,128)(2,1)}), bf16[448,368]{1,0:T(8,128)(2,1)}) %reduce-scatter.45.cloned.1.call-update) | async-done | bytes 329744
  686.1 31.3 %reduce-scatter.47.cloned.1.call-done = bf16[448,368]{1,0:T(8,128)(2,1)} async-done(((bf16[1792,368]{1,0:T(8,128)(2,1)}), bf16[448,368]{1,0:T(8,128)(2,1)}) %reduce-scatter.47.cloned.1.call-update) | async-done | bytes 329744
  719.6 31.1 %reduce-scatter.49.cloned.1.call-done = bf16[448,368]{1,0:T(8,128)(2,1)} async-done(((bf16[1792,368]{1,0:T(8,128)(2,1)}), bf16[448,368]{1,0:T(8,128)(2,1)}) %reduce-scatter.49.cloned.1.call-update) | async-done | bytes 329744
  (201 shorter events, 38.7 us)
Async XLA Ops:
  7.2 2.5 copy-start.26
  7.2 3.6 copy-start.28
  7.2 4.2 copy-start.31
  7.2 4.4 copy-start.34
  7.2 5.0 copy-start.33
  7.2 5.6 copy-start.18
  7.2 93.7 %reduce-scatter.29.cloned.1.call-start = ((), (), s32[]{:S(2)}) async-start(), calls=%async_computation.13 | async-start | bytes 2359296 | tf_op jit(solution)/shard_map/reduce_scatter | solution.py:408
  9.7 4.3 copy-start.15
  9.7 5.4 copy-start.17
  12.8 3.5 copy-start.14
  13.9 4.1 copy-start.40
  18.6 55.2 %slice-start = ((s8[5275648]{0:T(1024)(128)(4,1)}), s8[1081344]{0:T(1024)(128)(4,1)S(1)}, s32[]{:S(2)}) async-start(s8[5275648]{0:T(1024)(128)(4,1)} %bitcast.184), calls=%async_computation.26 | async-start | bytes 2162688
  67.7 6.2 slice-start.1
  67.7 6.2 copy-start.41
  67.7 9.2 %slice-start.2 = ((s8[5275648]{0:T(1024)(128)(4,1)}), s8[4194304]{0:T(1024)(128)(4,1)S(1)}, s32[]{:S(2)}) async-start(s8[5275648]{0:T(1024)(128)(4,1)} %bitcast.186), calls=%async_computation.28 | async-start | bytes 8388608
  73.8 3.1 slice-start.3
  85.0 3.0 copy-start.43
  85.0 3.0 copy-start.44
  91.0 1.7 copy-start.2
  92.6 28.0 %all-gather.2.cloned.1.call-start = ((), (), s32[]{:S(2)}) async-start(), calls=%async_computation.14 | async-start | bytes 2260992 | tf_op jit(solution)/shard_map/all_gather | solution.py:419
  92.7 10.5 %copy-start.7 = (bf16[1,256,1472]{2,1,0:T(8,128)(2,1)S(1)}, bf16[1,256,1472]{2,1,0:T(8,128)(2,1)}, u32[]{:S(2)}) copy-start(bf16[1,256,1472]{2,1,0:T(8,128)(2,1)} %copy.191) | copy-start | bytes 2260996
  92.9 10.9 %copy-start.36 = (f32[256]{0:T(256)}, f32[256]{0:T(256)S(1)}, u32[]{:S(2)}) copy-start(f32[256]{0:T(256)S(1)} %fusion.54) | copy-start | bytes 3076
  100.9 2.3 copy-start.9
  103.3 0.6 copy-start.38
  103.8 1.7 copy-start.20
  105.0 95.1 %reduce-scatter.31.cloned.1.call-start = ((), (), s32[]{:S(2)}) async-start(), calls=%async_computation.15 | async-start | bytes 983040 | tf_op jit(solution)/shard_map/reduce_scatter | solution.py:445
  106.2 1.7 copy-start.22
  106.2 3.7 copy-start.27
  107.8 2.2 copy-start.21
  120.7 2.3 copy-start.29
  120.7 2.2 copy-start.24
  120.7 2.3 copy-start.12
  120.7 2.3 copy-start.13
  129.7 1.9 copy-start
  131.6 71.8 %reduce-scatter.33.cloned.1.call-start = ((), (), s32[]{:S(2)}) async-start(), calls=%async_computation.16 | async-start | bytes 983040 | tf_op jit(solution)/shard_map/reduce_scatter | solution.py:448
  173.3 369.4 %all-reduce.14.cloned.1.call-start = ((), (), s32[]{:S(2)}) async-start(), calls=%async_computation.25 | async-start | bytes 36175872
  180.6 11.1 %copy-start.1 = (bf16[2,3,256,1024]{3,2,1,0:T(8,128)(2,1)S(1)}, bf16[2,3,256,1024]{3,2,1,0:T(8,128)(2,1)}, u32[]{:S(2)}) copy-start(bf16[2,3,256,1024]{3,2,1,0:T(8,128)(2,1)} %copy-done) | copy-start | bytes 9437188
  191.7 2.3 copy-start.5
  194.5 2.0 copy-start.11
  198.1 2.0 copy-start.6
  206.9 1.1 copy-start.19
  206.9 1.7 copy-start.16
  206.9 1.7 copy-start.25
  206.9 404.1 %reduce-scatter.35.cloned.1.call-start = ((), (), s32[]{:S(2)}) async-start(), calls=%async_computation.17 | async-start | bytes 2359296 | tf_op jit(solution)/shard_map/reduce_scatter | solution.py:464
  210.8 2.4 copy-start.23
  216.3 396.6 %reduce-scatter.27.cloned.1.call-start = ((), (), s32[]{:S(2)}) async-start(), calls=%async_computation.12 | async-start | bytes 2359296 | tf_op jit(solution)/shard_map/reduce_scatter | solution.py:395
  222.8 1.7 copy-start.42
  224.4 438.3 %reduce-scatter.37.cloned.1.call-start = ((), (), s32[]{:S(2)}) async-start(), calls=%async_computation.18 | async-start | bytes 184320
  544.6 119.7 %reduce-scatter.39.cloned.1.call-start = ((), (), s32[]{:S(2)}) async-start(), calls=%async_computation.19 | async-start | bytes 184320
  546.5 119.4 %reduce-scatter.41.cloned.1.call-start = ((), (), s32[]{:S(2)}) async-start(), calls=%async_computation.20 | async-start | bytes 184320
  548.4 119.1 %reduce-scatter.43.cloned.1.call-start = ((), (), s32[]{:S(2)}) async-start(), calls=%async_computation.21 | async-start | bytes 184320
  550.4 133.6 %reduce-scatter.45.cloned.1.call-start = ((), (), s32[]{:S(2)}) async-start(), calls=%async_computation.22 | async-start | bytes 1720320
  555.9 161.6 %reduce-scatter.47.cloned.1.call-start = ((), (), s32[]{:S(2)}) async-start(), calls=%async_computation.23 | async-start | bytes 1720320
  560.5 190.3 %reduce-scatter.49.cloned.1.call-start = ((), (), s32[]{:S(2)}) async-start(), calls=%async_computation.24 | async-start | bytes 1720320
  563.6 1.6 copy-start.35
  563.6 1.6 copy-start.32
  563.7 1.7 copy-start.4
  607.8 5.1 copy-start.8
  607.8 5.1 copy-start.37
  607.8 5.1 copy-start.39
  610.2 2.7 copy-start.3
  617.0 3.1 copy-start.10
  620.2 1.6 copy-start.30
Sparse Core Ops, SparseCore 0:
  92.7 8.1 reduce-scatter.28
  105.1 10.9 all-gather.1
  131.8 24.4 reduce-scatter.30
  173.4 24.4 reduce-scatter.32
  207.0 335.5 all-reduce.13
  544.8 10.0 reduce-scatter.34
  557.2 10.2 reduce-scatter.26
  570.3 20.4 reduce-scatter.36
  593.8 17.4 reduce-scatter.38
  613.9 17.5 reduce-scatter.40
  633.8 17.5 reduce-scatter.42
  653.6 30.2 reduce-scatter.44
  686.3 31.0 reduce-scatter.46
  719.6 31.0 reduce-scatter.48
